TPU v7x, 256 devices: a whole 4x4x8 slice. The times are simulated.
256 devices in a mesh: img: 16 (over y, z_lo, core), txt: 16 (over z_hi, x).
Axes of the slice: x: 4, y: 4, z: 8 (z_hi: 4, z_lo: 2; z = z_hi * 2 + z_lo), core: 2. Of those that a mesh axis runs over, the one named last changes fastest.
Arguments:
- image_emb: bfloat16 [16384, 1152], P(('img', 'txt')), may hold values from -64 to 64
- report_emb: bfloat16 [16384, 1152], P(('txt', 'img')), may hold values from -64 to 64
Outputs:
- grad_images: float32 [16384, 1152], P(('img', 'txt'))
- grad_reports: float32 [16384, 1152], P(('txt', 'img'))
- row_loss: float32 [16384], P(('img', 'txt'))
All inputs are finite; a program needn't handle non-finite values.
Results may differ from a plain program's by a relative error of at most 0.0078.
Values may be sent and summed in bfloat16 or wider, within the bound.
A program may use at most 64 MiB of HBM per device.

v0:
```python
import jax
import jax.numpy as jnp
from jax import lax
from jax.sharding import PartitionSpec as P

logit_scale = 100.0
logit_bias = -12.0


def unit_rows(values):
    wide = values.astype(jnp.float32)
    inverse = lax.rsqrt(jnp.sum(wide * wide, axis=1, keepdims=True) + 1e-06)
    return ((wide * inverse).astype(jnp.bfloat16), wide * inverse, inverse)


def pair_tile(img_block, rep_block, img_ids, rep_ids):
    logits = (
        logit_scale
        * lax.dot_general(
            img_block, rep_block, (((1,), (1,)), ((), ())), preferred_element_type=jnp.float32
        )
        + logit_bias
    )
    matches = (img_ids[:, None] == rep_ids[None, :]).astype(jnp.float32)
    losses = jax.nn.softplus(-(2.0 * matches - 1.0) * logits)
    slopes = (jax.nn.sigmoid(logits) - matches).astype(jnp.bfloat16)
    g_img = logit_scale * jnp.dot(slopes, rep_block, preferred_element_type=jnp.float32)
    g_rep = logit_scale * lax.dot_general(
        slopes, img_block, (((0,), (0,)), ((), ())), preferred_element_type=jnp.float32
    )
    return (jnp.sum(losses, axis=1), g_img, g_rep)


def project_back(grads, unit_wide, inverse):
    return inverse * (grads - unit_wide * jnp.sum(unit_wide * grads, axis=1, keepdims=True))


def on_device(image_emb, report_emb):
    own_img, wide_img, inv_img = unit_rows(image_emb)
    own_rep, wide_rep, inv_rep = unit_rows(report_emb)
    send_img, send_rep = (own_img, own_rep)
    rows_dev = image_emb.shape[0]
    img_rows = rows_dev * lax.axis_size("txt")
    rep_rows = rows_dev * lax.axis_size("img")
    img_first = lax.axis_index("img") * img_rows
    rep_first = lax.axis_index("txt") * rep_rows
    img_ids = img_first + jnp.arange(img_rows, dtype=jnp.int32)
    all_img = lax.all_gather(send_img, "txt", axis=0, tiled=True)
    piece = lax.all_gather(send_rep, "img", axis=0, tiled=True)
    count = piece.shape[0]
    piece_ids = rep_first + jnp.arange(count, dtype=jnp.int32)
    losses, g_img, g_rep = pair_tile(all_img, piece, img_ids, piece_ids)
    grep_own = lax.psum_scatter(g_rep, "img", scatter_dimension=0, tiled=True)
    gimg_own, row_loss = (
        lax.psum_scatter(g_img, "txt", scatter_dimension=0, tiled=True),
        lax.psum_scatter(losses, "txt", scatter_dimension=0, tiled=True),
    )
    return (
        project_back(gimg_own, wide_img, inv_img),
        project_back(grep_own, wide_rep, inv_rep),
        row_loss,
    )


def solution(mesh):
    in_specs = (P(("img", "txt"), None), P(("txt", "img"), None))
    out_specs = (P(("img", "txt"), None), P(("txt", "img"), None), P(("img", "txt")))
    return jax.shard_map(
        on_device, mesh=mesh, in_specs=in_specs, out_specs=out_specs, check_vma=False
    )
```

profile of v0, /device:TPU:1, one launch (start us, length us, event | category | flops | bytes accessed | tf_op | source)
XLA Modules:
  0.0 312.6 jit_solution(14443872456628612671)
XLA Ops:
  7.2 1.0 fusion.15
  8.3 1.7 fusion.11
  10.0 0.0 all-gather.5.cloned.1.call-start
  10.0 1.0 fusion.19
  11.1 1.7 fusion.8
  12.8 0.0 reduce-scatter.5.cloned.1.call-start
  12.8 63.2 %all-gather.3.cloned.1.call-done = bf16[1024,1152]{1,0:T(8,128)(2,1)} async-done(((bf16[64,1152]{1,0:T(8,128)(2,1)}), bf16[1024,1152]{1,0:T(8,128)(2,1)}) %all-gather.3.cloned.1.call-update) | async-done | bytes 2359312 | tf_op jit(solution)/shard_map/all_gather | solution.py:48
  76.0 38.0 %all-gather.5.cloned.1.call-done = bf16[1024,1152]{1,0:T(8,128)(2,1)} async-done(((bf16[64,1152]{1,0:T(8,128)(2,1)}), bf16[1024,1152]{1,0:T(8,128)(2,1)}) %all-gather.5.cloned.1.call-update) | async-done | bytes 2359312 | tf_op jit(solution)/shard_map/all_gather | solution.py:49
  114.0 8.0 %fusion.5 = (f32[1024]{0:T(1024)S(1)}, f32[1024,1024]{0,1:T(8,128)S(1)}) fusion(s32[1024]{0:T(1024)S(1)} %get-tuple-element.6, s32[1024]{0:T(1024)S(1)} %get-tuple-element.5, bf16[1024,1152]{1,0:T(8,128)(2,1)} %all-gather.3.cloned.1.call-done, bf16[1024,1152]{1,0:T(8,128)(2,1)} %all-gather.5.cloned.1.call-done), kind=kOutput, calls=%fused_computation.10 | convolution fusion | flops 2430598144 | bytes 8925184 | tf_op jit(solution)/shard_map/dot_general | solution.py:19
  122.0 2.1 copy-done.5
  124.1 5.4 %convolution_multiply_fusion = f32[1024,1152]{1,0:T(8,128)} fusion(bf16[1024,1152]{1,0:T(8,128)(2,1)S(1)} %copy-done.2, f32[1024,1024]{0,1:T(8,128)S(1)} %get-tuple-element.4, s32[1024]{0:T(1024)S(1)} %get-tuple-element.6, s32[1024]{0:T(1024)S(1)} %get-tuple-element.5), kind=kOutput, calls=%fused_computation.3 | convolution fusion | flops 2426535936 | bytes 11280384 | tf_op jit(solution)/shard_map/dot_general | solution.py:28
  129.5 0.0 reduce-scatter.3.cloned.1.call-start
  129.6 1.6 copy-done.3
  131.1 7.8 %convolution_multiply_fusion.1 = f32[1024,1152]{1,0:T(8,128)} fusion(bf16[1024,1152]{1,0:T(8,128)(2,1)S(1)} %copy-done.3, f32[1024,1024]{0,1:T(8,128)} %copy-done.5, s32[1024]{0:T(1024)S(1)} %get-tuple-element.6, s32[1024]{0:T(1024)S(1)} %get-tuple-element.5), kind=kOutput, calls=%fused_computation.4 | convolution fusion | flops 2426535936 | bytes 11280384 | tf_op jit(solution)/shard_map/dot_general | solution.py:27
  139.0 0.6 copy-done.4
  139.7 0.6 dynamic-slice
  140.9 38.2 %all-reduce = f32[1024]{0:T(1024)S(1)} all-reduce(f32[1024]{0:T(1024)S(1)} %get-tuple-element.3), channel_id=4, replica_groups=mesh['img'=16,'txt'=16] {'txt'}, use_global_device_ids=true, to_apply=%region_7.8.clone | all-reduce | flops 1024 | bytes 8192
  179.1 0.6 dynamic-slice.1
  179.7 21.8 %reduce-scatter.5.cloned.1.call-done = f32[64,1152]{1,0:T(8,128)} async-done(((f32[1024,1152]{1,0:T(8,128)}), f32[64,1152]{1,0:T(8,128)}) %reduce-scatter.5.cloned.1.call-update) | async-done | bytes 294928 | tf_op jit(solution)/shard_map/reduce_scatter | solution.py:53
  201.5 1.2 fusion.16
  202.7 1.8 fusion.18
  204.5 98.6 %reduce-scatter.3.cloned.1.call-done = f32[64,1152]{1,0:T(8,128)} async-done(((f32[1024,1152]{1,0:T(8,128)}), f32[64,1152]{1,0:T(8,128)}) %reduce-scatter.3.cloned.1.call-update) | async-done | bytes 294928 | tf_op jit(solution)/shard_map/reduce_scatter | solution.py:55
  303.1 1.2 fusion.12
  304.3 1.8 fusion.14
  (17 shorter events, 0.1 us)
Async XLA Ops:
  7.2 68.8 %all-gather.3.cloned.1.call-start = ((), (), s32[]{:S(2)}) async-start(), calls=%async_computation.2 | async-start | bytes 2506752 | tf_op jit(solution)/shard_map/all_gather | solution.py:48
  10.0 104.0 %all-gather.5.cloned.1.call-start = ((), (), s32[]{:S(2)}) async-start(), calls=%async_computation.3 | async-start | bytes 2506752 | tf_op jit(solution)/shard_map/all_gather | solution.py:49
  12.8 188.7 %reduce-scatter.5.cloned.1.call-start = ((), (), s32[]{:S(2)}) async-start(), calls=%async_computation.5 | async-start | bytes 5013504 | tf_op jit(solution)/shard_map/reduce_scatter | solution.py:53
  114.0 10.1 %copy-start.2 = (bf16[1024,1152]{1,0:T(8,128)(2,1)S(1)}, bf16[1024,1152]{1,0:T(8,128)(2,1)}, u32[]{:S(2)}) copy-start(bf16[1024,1152]{1,0:T(8,128)(2,1)} %all-gather.3.cloned.1.call-done) | copy-start | bytes 7077892
  122.0 2.1 copy-start.5
  129.5 1.7 copy-start.3
  129.5 173.6 %reduce-scatter.3.cloned.1.call-start = ((), (), s32[]{:S(2)}) async-start(), calls=%async_computation.4 | async-start | bytes 5013504 | tf_op jit(solution)/shard_map/reduce_scatter | solution.py:55
  139.0 0.7 copy-start.4
  139.0 62.5 %copy-start = (bf16[64,1152]{1,0:T(8,128)(2,1)S(1)}, bf16[64,1152]{1,0:T(8,128)(2,1)}, u32[]{:S(2)}) copy-start(bf16[64,1152]{1,0:T(8,128)(2,1)} %param.3) | copy-start | bytes 442372
  139.0 164.1 %copy-start.1 = (bf16[64,1152]{1,0:T(8,128)(2,1)S(1)}, bf16[64,1152]{1,0:T(8,128)(2,1)}, u32[]{:S(2)}) copy-start(bf16[64,1152]{1,0:T(8,128)(2,1)} %param.2) | copy-start | bytes 442372
Sparse Core Ops, SparseCore 0:
  11.0 64.9 all-gather.2
  78.4 35.5 all-gather.4
  129.6 71.8 reduce-scatter.4
  205.0 98.0 reduce-scatter.2
where the time goes:
time: 313 us
  waiting for transfers between devices  222 us (71%)
  blocking collectives  38.2 us (12%)
  matrix products  21.2 us (7%)
  between operations  14.5 us (5%)
  other arithmetic  11.4 us (4%)
  local copies, waits for them, and re-layouts  5.48 us (2%)
    reduce_scatter x1, waiting for transfers between devices, on_device(): lax.psum_scatter(g_img, 'txt', scatter_dimension=0, tiled=True)  98.6 us
    all_gather x1, waiting for transfers between devices, on_device(): all_img = lax.all_gather(send_img, 'txt', axis=0, tiled=True)  63.2 us
    unnamed x1, blocking collectives  38.2 us
    all_gather x1, waiting for transfers between devices, on_device(): piece = lax.all_gather(send_rep, 'img', axis=0, tiled=True)  38 us
    reduce_scatter x1, waiting for transfers between devices, on_device(): grep_own = lax.psum_scatter(g_rep, 'img', scatter_dimension=0, tiled=True)  21.8 us
    dot_general x1, matrix products, pair_tile(): lax.dot_general(img_block, rep_block, (((1,), (1,)), ((), ())), preferred...  8 us
    dot_general x1, matrix products, pair_tile(): jnp.dot(slopes, rep_block, preferred_element_type=jnp.float32)  7.84 us
  transfers between devices with their start and end apart: 4, of which 4 were waited for; matrix products, arithmetic and copies ran while one was open for 5% of the time, Pallas kernels for 0%

commit v1 on v0

v1 whole, which is shorter than its diff:
```python
import functools

import jax
import jax.numpy as jnp
from jax import lax
from jax.experimental import pallas as pl
from jax.experimental.pallas import tpu as pltpu
from jax.sharding import PartitionSpec as P

MESH = pl.DeviceIdType.MESH
F32, BF16 = jnp.float32, jnp.bfloat16
logit_scale = 100.0
logit_bias = -12.0
D = 1152
X, Y, Z, C = range(4)
SIZES = (4, 4, 8, 2)

IMG_AT = [(0, 0), (1, 0), (3, 0), (0, 1), (0, 3), (1, 1), (1, 3), (3, 1), (3, 3), (2, 0), (0, 2), (2, 1), (2, 3), (1, 2), (3, 2), (2, 2)]
IMG_POS = {o: n for n, o in enumerate(IMG_AT)}
REP_AT = [0, 1, 7, 2, 6, 3, 5, 4]
REP_POS = {o: n for n, o in enumerate(REP_AT)}
TABLE_X = sum(o[0] << (2 * n) for n, o in enumerate(IMG_AT))
TABLE_Y = sum(o[1] << (2 * n) for n, o in enumerate(IMG_AT))
TABLE_Z = sum(o << (3 * n) for n, o in enumerate(REP_AT))
JS = (2, 1, 3, 0)


def signed(table):
    return table - (1 << 32) if table >= 1 << 31 else table


def my_coords():
    i, t = lax.axis_index("img"), lax.axis_index("txt")
    x, z_hi = lax.rem(t, 4), lax.div(t, 4)
    y, z_lo, c = lax.div(i, 4), lax.rem(lax.div(i, 2), 2), lax.rem(i, 2)
    return (x, y, z_hi * 2 + z_lo, c)


def device_at(co, axis, step):
    co = list(co)
    co[axis] = lax.rem(co[axis] + step + SIZES[axis], SIZES[axis])
    x, y, z, c = co
    return (y * 4 + lax.rem(z, 2) * 2 + c, lax.div(z, 2) * 4 + x)


def rows(first, count):
    return pl.ds(first, count)


def unit_rows(ref):
    wide = ref[...].astype(F32)
    inverse = lax.rsqrt(jnp.sum(wide * wide, axis=1, keepdims=True) + 1e-06)
    return wide * inverse, inverse


def project_back(grads, unit_wide, inverse):
    return inverse * (grads - unit_wide * jnp.sum(unit_wide * grads, axis=1, keepdims=True))


def kernel(
    img_ref, rep_ref, gimg_ref, grep_ref, loss_ref,
    ibuf, rbuf, slopes, slopes_t, lacc, gr, ga1, gy,
    st_c, ld_c, st_z, ld_z, st1, ld1, st2, ld2, lb_s, lb_l, lw_s, lw_l,
    ssem, rsem,
):
    me = my_coords()
    peers = [(X, 1), (X, -1), (X, 2), (Y, 1), (Y, -1), (Y, 2), (Z, 1), (Z, -1), (C, 1)]
    barrier = pltpu.get_barrier_semaphore()
    for axis, step in peers:
        pl.semaphore_signal(barrier, inc=1, device_id=device_at(me, axis, step), device_id_type=MESH)

    unit_img, _ = unit_rows(img_ref)
    ibuf[0] = unit_img.astype(BF16)
    unit_rep, _ = unit_rows(rep_ref)
    rbuf[0, 0] = unit_rep.astype(BF16)
    lacc[...] = jnp.zeros_like(lacc)
    pl.semaphore_wait(barrier, len(peers))

    started = []
    count = [0]

    def copy(src, dst, axis, step):
        k = count[0]
        count[0] += 1
        return pltpu.make_async_remote_copy(
            src, dst, ssem.at[k], rsem.at[k], device_id=device_at(me, axis, step), device_id_type=MESH
        )

    def start(*copies):
        for one in copies:
            one.start()
            started.append(one)

    def arrive(*copies):
        for one in copies:
            one.wait_recv()

    def shift(o, axis, by):
        o = list(o)
        o[axis] = (o[axis] + by) % 4
        return tuple(o)

    def img_copy(o, part, axis, step):
        return copy(
            ibuf.at[IMG_POS[o], part], ibuf.at[IMG_POS[shift(o, axis, -step)], part], axis, step
        )

    halves = [rows(0, 32), rows(32, 32)]
    quarters = [[rows(0, 16), rows(16, 16)], [rows(32, 16), rows(48, 16)]]
    SIGNS = (1, -1)
    own = (0, 0)
    g1, g2, g3, g4 = {}, {}, {}, {}
    for h in (0, 1):
        p, q = h, 1 - h
        for s in SIGNS:
            qs = quarters[h][0 if s == 1 else 1]
            g1[h, s] = img_copy(own, halves[h], p, s)
            g2[h, s] = img_copy(shift(own, p, -s), qs, p, s)
            for j in (0, 1, 3, 2):
                g3[h, s, j] = img_copy(shift(own, p, j), halves[h], q, s)
                g4[h, s, j] = img_copy(shift(shift(own, p, j), q, -s), qs, q, s)

    chunks = [rows(0, 32), rows(32, 32)]

    def rep_copy(o, part, step):
        return copy(
            rbuf.at[REP_POS[o % 8], 0, part], rbuf.at[REP_POS[(o - step) % 8], 0, part], Z, step
        )

    zg = {}
    for s in SIGNS:
        first = 0 if s == 1 else 1
        for d in (1, 2, 3):
            for n in (first, 1 - first):
                zg[d, s, n] = rep_copy(-s * (d - 1), chunks[n], s)
        zg[4, s, first] = rep_copy(-s * 3, chunks[first], s)
    cg = {o: copy(rbuf.at[REP_POS[o], 0], rbuf.at[REP_POS[o], 1], C, 1) for o in REP_AT}

    matched = jnp.logical_and(me[Y] == lax.div(me[Z], 2), me[X] == lax.rem(me[Z], 2) * 2 + me[C])
    aside = jnp.where(matched, 0, 1 << 20)
    row_in = lax.broadcasted_iota(jnp.int32, (64, 1), 0)
    col_in = lax.broadcasted_iota(jnp.int32, (1, 128), 1)

    def tile(a, b):
        lhs = ibuf[pl.ds(a * 4, 4)].reshape(256, D)
        rhs = rbuf[pl.ds(b * 2, 2)].reshape(256, D)
        logits = logit_scale * lax.dot_general(
            lhs, rhs, (((1,), (1,)), ((), ())), preferred_element_type=F32
        ) + logit_bias
        row_ids, col_ids = [], []
        for k in range(4):
            n = (a * 4 + k) * 2
            bx = lax.rem((lax.shift_right_logical(jnp.int32(signed(TABLE_X)), n) & 3) + me[X], 4)
            by = lax.rem((lax.shift_right_logical(jnp.int32(signed(TABLE_Y)), n) & 3) + me[Y], 4)
            row_ids.append((by * 4 + bx) * 64 + aside + row_in)
        for k in range(2):
            bz = lax.rem((lax.shift_right_logical(jnp.int32(TABLE_Z), (b * 2 + k) * 3) & 7) + me[Z], 8)
            mine = (bz * 2 + me[C]) * 64
            other = (bz * 2 + 1 - me[C]) * 64
            col_ids.append(jnp.where(col_in < 64, mine + col_in, other + col_in - 64))
        matches = jnp.concatenate(row_ids, axis=0) == jnp.concatenate(col_ids, axis=1)
        e = jnp.exp(-jnp.abs(logits))
        r = 1.0 / (1.0 + e)
        sig = jnp.where(logits >= 0, r, e * r)
        losses = jnp.maximum(logits, 0.0) + jnp.log1p(e)
        losses = jnp.where(matches, losses - logits, losses)
        sl32 = jnp.where(matches, sig - 1.0, sig)
        sl = sl32.astype(BF16)
        slopes[pl.ds(a * 4, 4), :, pl.ds(pl.multiple_of(b * 256, 256), 256)] = sl.reshape(4, 64, 256)
        slopes_t[pl.ds(b * 2, 2), :, pl.ds(pl.multiple_of(a * 256, 256), 256)] = sl.T.reshape(2, 128, 256)
        lacc[pl.ds(a * 4, 4)] += (losses[:, :128] + losses[:, 128:]).reshape(4, 64, 128)

    def tiles(pairs):
        if len(pairs) == 1:
            tile(*pairs[0])
            return
        ta = sum(a << (2 * n) for n, (a, _) in enumerate(pairs))
        tb = sum(b << (2 * n) for n, (_, b) in enumerate(pairs))

        def body(n, carry):
            tile(
                lax.shift_right_logical(jnp.int32(ta), n * 2) & 3,
                lax.shift_right_logical(jnp.int32(tb), n * 2) & 3,
            )
            return carry

        lax.fori_loop(0, len(pairs), body, 0)

    for h in (0, 1):
        start(g1[h, 1], g1[h, -1])
    start(zg[1, 1, 0], zg[1, -1, 1], zg[1, 1, 1], zg[1, -1, 0])
    for h in (0, 1):
        start(g3[h, 1, 0], g3[h, -1, 0])
    start(cg[0])

    for h in (0, 1):
        for s in SIGNS:
            arrive(g1[h, s])
            start(g2[h, s])
    for n in (0, 1):
        for s in SIGNS:
            m = n if s == 1 else 1 - n
            arrive(zg[1, s, m])
            start(zg[2, s, m])
    for h in (0, 1):
        for j in (1, 3):
            start(g3[h, 1, j], g3[h, -1, j])
    start(cg[1], cg[7])
    for h in (0, 1):
        for s in SIGNS:
            arrive(g3[h, s, 0])
            start(g4[h, s, 0])
    arrive(cg[0], cg[1])
    tiles([(0, 0)])
    for h in (0, 1):
        arrive(g2[h, 1], g2[h, -1])
        start(g3[h, 1, 2], g3[h, -1, 2])
    for n in (0, 1):
        for s in SIGNS:
            m = n if s == 1 else 1 - n
            arrive(zg[2, s, m])
            start(zg[3, s, m])
    start(cg[2], cg[6])
    for h in (0, 1):
        for j in (1, 3):
            for s in SIGNS:
                arrive(g3[h, s, j])
                start(g4[h, s, j])
    arrive(cg[7], cg[2])
    tiles([(0, 1), (1, 0), (1, 1)])
    for s in SIGNS:
        m = 0 if s == 1 else 1
        arrive(zg[3, s, m])
        start(zg[4, s, m])
    for s in SIGNS:
        m = 1 if s == 1 else 0
        arrive(zg[3, s, m])
    start(cg[3], cg[5])
    for h in (0, 1):
        for s in SIGNS:
            arrive(g3[h, s, 2])
            start(g4[h, s, 2])
    for h in (0, 1):
        arrive(g4[h, 1, 0], g4[h, -1, 0])
    arrive(g4[1, 1, 1], g4[1, -1, 1])
    arrive(cg[6], cg[3])
    tiles([(0, 2), (1, 2), (2, 0), (2, 1), (2, 2)])
    arrive(zg[4, 1, 0], zg[4, -1, 1])
    start(cg[4])
    for h in (0, 1):
        for j in (1, 3, 2):
            if (h, j) != (1, 1):
                arrive(g4[h, 1, j], g4[h, -1, j])
    tiles([(3, 0), (3, 1), (3, 2)])
    arrive(cg[5], cg[4])
    tiles([(0, 3), (1, 3), (2, 3), (3, 3)])

    def at(h, j, dq):
        return (j, dq % 4) if h == 0 else (dq % 4, j)

    def img_terms(pieces):
        lhs = jnp.concatenate([slopes[IMG_POS[at(*n)], halves[n[0]]] for n in pieces], axis=0)
        rhs = rbuf[...].reshape(1024, D)
        return logit_scale * jnp.dot(lhs, rhs, preferred_element_type=F32)

    def rep_terms(offsets):
        lhs = jnp.concatenate([slopes_t[REP_POS[o]] for o in offsets], axis=0)
        rhs = ibuf[...].reshape(1024, D)
        out = logit_scale * jnp.dot(lhs, rhs, preferred_element_type=F32)
        for n, o in enumerate(offsets):
            gr[REP_POS[o]] = out[n * 128 : n * 128 + 64]
            st_c[REP_POS[o]] = out[n * 128 + 64 : n * 128 + 128].astype(BF16)

    r1, r2, rz, lx, ly = {}, {}, {}, {}, {}
    for h in (0, 1):
        p, q = h, 1 - h
        for n, s in enumerate(SIGNS):
            for slot in range(3):
                groups = [rows(0, 4)] if slot == 0 else [rows(0, 3), rows(3, 1)]
                for g, part in enumerate(groups):
                    r1[h, s, slot, g] = copy(st1.at[h, n, slot, part], ld1.at[h, n, slot, part], q, s)
                r2[h, s, slot] = copy(st2.at[h, n, slot], ld2.at[h, n, slot], p, s)
    for n, s in enumerate(SIGNS):
        for slot in range(7):
            rz[s, slot] = copy(st_z.at[n, slot], ld_z.at[n, slot], Z, s)
    cr = {o: copy(st_c.at[REP_POS[o]], ld_c.at[REP_POS[o]], C, 1) for o in REP_AT}
    for d, step in ((1, 1), (2, 2), (3, -1)):
        lx[d] = copy(lb_s.at[d], lb_l.at[d], X, step)
        ly[d] = copy(lw_s, lw_l.at[d], Y, step)

    def first_out(h, out, at_row):
        for k in range(4):
            for n in (0, 1):
                st1[h, n, 0, k] = out[at_row + k * 32 + n * 16 : at_row + k * 32 + n * 16 + 16].astype(BF16)

    def second_out(h, out):
        for n in (0, 1):
            for k in range(4):
                base = (n * 4 + k) * 32
                quarter = [out[base : base + 16], out[base + 16 : base + 32]]
                st1[h, n, 1, k] = quarter[1 - n].astype(BF16)
                ga1[h, n, k] = quarter[n]

    def carry_on(h, g):
        for n, s in enumerate(SIGNS):
            if g == 0:
                arrive(r1[h, s, 0, 0])
            for k in (0, 1, 2) if g == 0 else (3,):
                st1[h, n, 2, k] = (ga1[h, n, k] + ld1[h, n, 0, k].astype(F32)).astype(BF16)
            start(r1[h, s, 2, g])

    def paired(o, part):
        return gr[REP_POS[o % 8], part] + ld_c[REP_POS[o % 8], part].astype(F32)

    def z_send(slot):
        d = 4 - (slot + 1) // 2
        for n, s in enumerate(SIGNS):
            carried = slot % 2 == 0
            part = chunks[n] if carried else chunks[1 - n]
            term = paired(s * d, part)
            if slot >= 2:
                arrive(rz[s, slot - 2])
                term = term + ld_z[n, slot - 2].astype(F32)
            st_z[n, slot] = term.astype(BF16)
            start(rz[s, slot])

    out = img_terms([(h, j, 2) for h in (0, 1) for j in JS])
    for h in (0, 1):
        first_out(h, out, h * 128)
        start(r1[h, 1, 0, 0], r1[h, -1, 0, 0])
    rep_terms([4, 0])
    start(cr[4], cr[0])
    for h in (0, 1):
        second_out(h, img_terms([(h, j, s) for s in SIGNS for j in JS]))
        for s in SIGNS:
            start(r1[h, s, 1, 0])
        if h == 0:
            arrive(cr[4])
            z_send(0)
    rep_terms([3, 5])
    start(cr[3], cr[5])
    for h in (0, 1):
        carry_on(h, 0)
        start(r1[h, 1, 1, 1], r1[h, -1, 1, 1])
    rep_terms([2, 6])
    start(cr[2], cr[6])
    arrive(cr[3], cr[5])
    z_send(1)
    z_send(2)
    for h in (0, 1):
        carry_on(h, 1)
    rep_terms([1, 7])
    start(cr[1], cr[7])
    arrive(cr[2], cr[6])
    z_send(3)
    out = img_terms([(h, j, 0) for h in (0, 1) for j in JS])
    for h in (0, 1):
        for k in range(4):
            gy[h, k] = out[(h * 4 + k) * 32 : (h * 4 + k) * 32 + 32]

    lb_s[...] = jnp.zeros_like(lb_s)
    for k in range(8):
        line = jnp.sum(lacc[2 * k : 2 * k + 2].reshape(128, 128).T, axis=0, keepdims=True)
        for n in (0, 1):
            dx, dy = IMG_AT[2 * k + n]
            lb_s[dx, dy : dy + 1, :] = line if n == 0 else pltpu.roll(line, 64, 1)
    start(lx[1], lx[2], lx[3])
    z_send(4)

    arrive(lx[1], lx[2], lx[3])
    lw_s[...] = lb_s[0] + lb_l[1] + lb_l[2] + lb_l[3]
    start(ly[1], ly[2], ly[3])
    arrive(cr[1], cr[7])
    z_send(5)

    def line_sum(h, k, n):
        total = gy[h, k, n * 16 : n * 16 + 16]
        total = total + ld1[h, n, 2, k].astype(F32)
        return total + ld1[h, 1 - n, 1, k].astype(F32)

    for h in (0, 1):
        for s in SIGNS:
            arrive(r1[h, s, 1, 0], r1[h, s, 2, 0])
        for n, s in enumerate(SIGNS):
            st2[h, n, 0] = line_sum(h, 0, n).astype(BF16)
            start(r2[h, s, 0])
    for h in (0, 1):
        for n, s in enumerate(SIGNS):
            st2[h, n, 1] = line_sum(h, 1 + n, 1 - n).astype(BF16)
            start(r2[h, s, 1])
    z_send(6)
    for h in (0, 1):
        for n, s in enumerate(SIGNS):
            arrive(r2[h, s, 0])
            st2[h, n, 2] = (line_sum(h, 1 + n, n) + ld2[h, n, 0].astype(F32)).astype(BF16)
            start(r2[h, s, 2])

    arrive(ly[1], ly[2], ly[3])
    loss = lw_s[0:1, :]
    for d in (1, 2, 3):
        loss = loss + lw_l[d, d : d + 1, :]
    loss_ref[...] = jnp.broadcast_to(loss, loss_ref.shape)

    for n, s in enumerate(SIGNS):
        arrive(rz[s, 5], rz[s, 6])
    arrive(cr[0])
    unit_rep, inv_rep = unit_rows(rep_ref)
    halves_rep = []
    for n in (0, 1):
        total = paired(0, chunks[n]) + ld_z[n, 6].astype(F32) + ld_z[1 - n, 5].astype(F32)
        halves_rep.append(total)
    grep_ref[...] = project_back(jnp.concatenate(halves_rep, axis=0), unit_rep, inv_rep)

    quarter_sums = []
    for h in (0, 1):
        for s in SIGNS:
            arrive(r1[h, s, 1, 1], r1[h, s, 2, 1], r2[h, s, 1], r2[h, s, 2])
        for n in (0, 1):
            quarter_sums.append(
                line_sum(h, 3, n) + ld2[h, n, 2].astype(F32) + ld2[h, 1 - n, 1].astype(F32)
            )
    unit_img, inv_img = unit_rows(img_ref)
    gimg_ref[...] = project_back(jnp.concatenate(quarter_sums, axis=0), unit_img, inv_img)
    for one in started:
        one.wait_send()


COPIES = 40 + 14 + 8 + 20 + 12 + 14 + 8 + 6


def on_device(image_emb, report_emb):
    vmem = pl.BlockSpec(memory_space=pltpu.VMEM)
    gimg, grep, loss = pl.pallas_call(
        kernel,
        out_shape=(
            jax.ShapeDtypeStruct((64, D), F32),
            jax.ShapeDtypeStruct((64, D), F32),
            jax.ShapeDtypeStruct((8, 128), F32),
        ),
        in_specs=[vmem, vmem],
        out_specs=(vmem, vmem, vmem),
        scratch_shapes=[
            pltpu.VMEM((16, 64, D), BF16),
            pltpu.VMEM((8, 2, 64, D), BF16),
            pltpu.VMEM((16, 64, 1024), BF16),
            pltpu.VMEM((8, 128, 1024), BF16),
            pltpu.VMEM((16, 64, 128), F32),
            pltpu.VMEM((8, 64, D), F32),
            pltpu.VMEM((2, 2, 4, 16, D), F32),
            pltpu.VMEM((2, 4, 32, D), F32),
            pltpu.VMEM((8, 64, D), BF16),
            pltpu.VMEM((8, 64, D), BF16),
            pltpu.VMEM((2, 7, 32, D), BF16),
            pltpu.VMEM((2, 7, 32, D), BF16),
            pltpu.VMEM((2, 2, 3, 4, 16, D), BF16),
            pltpu.VMEM((2, 2, 3, 4, 16, D), BF16),
            pltpu.VMEM((2, 2, 3, 16, D), BF16),
            pltpu.VMEM((2, 2, 3, 16, D), BF16),
            pltpu.VMEM((4, 8, 128), F32),
            pltpu.VMEM((4, 8, 128), F32),
            pltpu.VMEM((8, 128), F32),
            pltpu.VMEM((4, 8, 128), F32),
            pltpu.SemaphoreType.DMA((COPIES,)),
            pltpu.SemaphoreType.DMA((COPIES,)),
        ],
        compiler_params=pltpu.CompilerParams(
            collective_id=0, has_side_effects=True, vmem_limit_bytes=56 * 2**20
        ),
        cost_estimate=pl.CostEstimate(
            flops=3 * 2 * 1024 * 1024 * D, bytes_accessed=900000, transcendentals=3 * 1024 * 1024
        ),
    )(image_emb, report_emb)
    return gimg, grep, loss[0, :64]


def solution(mesh):
    in_specs = (P(("img", "txt"), None), P(("txt", "img"), None))
    out_specs = (P(("img", "txt"), None), P(("txt", "img"), None), P(("img", "txt")))
    return jax.shard_map(
        on_device, mesh=mesh, in_specs=in_specs, out_specs=out_specs, check_vma=False
    )
```

time: 313 us -> 62.4 us (0.20)
  the two profiles are of different devices: /device:TPU:1 before, /device:TPU:2 now
where the time goes in v1:
time: 62.4 us; the launch traced here: 62.2 us
  Pallas kernels  57.9 us (93%)
  local copies, waits for them, and re-layouts  3.64 us (6%)
  between operations  0.64 us (1%)
    pallas_call x1, Pallas kernels, on_device(): pl.pallas_call(kernel, out_shape=(jax.ShapeDtypeStruct((64, D), F32), jax...  57.9 us
    unnamed x4, local copies, waits for them, and re-layouts  2.46 us

profile of v1, /device:TPU:2, one launch (start us, length us, event | category | flops | bytes accessed | tf_op | source)
XLA Modules:
  0.0 62.2 jit_solution(2332596241900644791)
XLA Ops:
  0.6 57.9 %shard_map.49 = (f32[64,1152]{1,0:T(8,128)}, f32[64,1152]{1,0:T(8,128)}, f32[8,128]{1,0:T(8,128)}) custom-call(bf16[64,1152]{1,0:T(8,128)(2,1)} %img_ref.1, bf16[64,1152]{1,0:T(8,128)(2,1)} %rep_ref.1), custom_call_target="tpu_custom_call" | custom-call | flops 7247757312 | bytes 900000 | tf_op jit(solution)/shard_map/pallas_call | solution.py:433
  58.6 1.2 %slice_bitcast_fusion = f32[64]{0:T(128)} fusion(f32[8,128]{1,0:T(8,128)} %get-tuple-element.8), kind=kLoop, calls=%fused_computation | loop fusion | bytes 512 | tf_op jit(solution)/shard_map/squeeze | solution.py:473
  59.8 0.0 copy-start
  59.8 1.7 %copy.7 = f32[64,1152]{1,0:T(8,128)} copy(f32[64,1152]{1,0:T(8,128)} %get-tuple-element.12) | data formatting | bytes 589824
  61.5 0.0 copy-done
  61.5 0.7 %copy.8 = f32[64,1152]{1,0:T(8,128)} copy(f32[64,1152]{1,0:T(8,128)S(1)} %copy-done) | data formatting | bytes 589824
Async XLA Ops:
  59.8 1.7 %copy-start = (f32[64,1152]{1,0:T(8,128)S(1)}, f32[64,1152]{1,0:T(8,128)}, u32[]{:S(2)}) copy-start(f32[64,1152]{1,0:T(8,128)} %get-tuple-element.13) | copy-start | bytes 884740

commit v2 on v0

v2 whole, which is shorter than its diff:
```python
import functools

import jax
import jax.numpy as jnp
from jax import lax
from jax.experimental import pallas as pl
from jax.experimental.pallas import tpu as pltpu
from jax.sharding import PartitionSpec as P

MESH = pl.DeviceIdType.MESH
F32, BF16 = jnp.float32, jnp.bfloat16
LOG2E, LN2 = 1.4426950408889634, 0.6931471805599453
logit_scale = 100.0
logit_bias = -12.0
D = 1152
X, Y, Z, C = range(4)
SIZES = (4, 4, 8, 2)
SIGNS = (1, -1)

IMG_AT = [(0, 0), (1, 0), (3, 0), (0, 1), (0, 3), (1, 1), (1, 3), (3, 1), (3, 3), (2, 0), (0, 2), (2, 1), (2, 3), (1, 2), (3, 2), (2, 2)]
REP_AT = [0, 1, 7, 2, 6, 3, 5, 4]
IMG_POS = {o: n for n, o in enumerate(IMG_AT)}
REP_POS = {o: n for n, o in enumerate(REP_AT)}
JS = (2, 1, 3, 0)
TILES = [(0, 4, 0, 4), (4, 4, 0, 4), (0, 8, 4, 2), (8, 4, 0, 6), (0, 12, 6, 2), (12, 4, 0, 8)]


def shift(o, axis, by):
    o = list(o)
    o[axis] = (o[axis] + by) % 4
    return tuple(o)


def at(h, j, dq):
    return (j, dq % 4) if h == 0 else (dq % 4, j)


def z_chunks(s):
    return (0, 1, 2, 3) if s == 1 else (2, 3, 0, 1)


def plan():
    steps = []

    def add(name, axis, step, rows, needs):
        steps.append((name, axis, step, rows, list(dict.fromkeys(needs))))
        return [name]

    img = {((0, 0), h, u): [] for h in (0, 1) for u in (0, 1)}
    for h in (0, 1):
        p, q = h, 1 - h
        for u in (0, 1):
            for s in SIGNS:
                img[shift((0, 0), p, -s), h, u] = add(("g1", h, s, u), p, s, 16, [])
        for n, s in enumerate(SIGNS):
            src = shift((0, 0), p, -s)
            img[shift(src, p, -s), h, n] = add(("g2", h, s), p, s, 16, img[src, h, n])
        for j in (0, 1, 3, 2):
            line = shift((0, 0), p, j)
            for u in (0, 1):
                for s in SIGNS:
                    img[shift(line, q, -s), h, u] = add(("g3", h, s, j, u), q, s, 16, img[line, h, u])
            for n, s in enumerate(SIGNS):
                src = shift(line, q, -s)
                img[shift(src, q, -s), h, n] = add(("g4", h, s, j), q, s, 16, img[src, h, n])
    rep = {(0, c): [] for c in range(4)}
    for s in SIGNS:
        for d in (1, 2, 3, 4):
            for c in z_chunks(s)[: 4 if d < 4 else 2]:
                rep[-s * d % 8, c] = add(("z", d, s, c), Z, s, 16, rep[-s * (d - 1) % 8, c])
    whole = {}
    for o in REP_AT:
        mine = [n for c in range(4) for n in rep[o, c]]
        whole[o] = mine + add(("cg", o), C, 1, 64, mine)
    cover = {}
    for i, ni, r, nr in TILES:
        needs = [n for k in range(i, i + ni) for h in (0, 1) for u in (0, 1) for n in img[IMG_AT[k], h, u]]
        needs += [n for k in range(r, r + nr) for n in whole[REP_AT[k]]]
        add(("tile", i, ni, r, nr), None, 0, ni * nr, needs)
        for k in range(i, i + ni):
            for m in range(r, r + nr):
                cover[k, m] = ("tile", i, ni, r, nr)
    img_tiles = lambda blocks: [cover[IMG_POS[o], m] for o in blocks for m in range(8)]
    rep_tiles = lambda blocks: [cover[k, REP_POS[o]] for o in blocks for k in range(16)]
    add("ig2", None, 0, 256, img_tiles([at(h, j, 2) for h in (0, 1) for j in JS]))
    for h in (0, 1):
        add(("ig1", h), None, 0, 256, img_tiles([at(h, j, s) for s in SIGNS for j in JS]))
    add("ig0", None, 0, 256, img_tiles([at(h, j, 0) for h in (0, 1) for j in JS]))
    for d in (4, 3, 2, 1):
        add(("rg", d), None, 0, 256, rep_tiles([d, 0] if d == 4 else [d, 8 - d]))
    for d in (4, 3, 2, 1, 0):
        for o in (d, 8 - d) if d in (1, 2, 3) else (d,):
            add(("cr", o), C, 1, 64, [("rg", d or 4)])
    for s in SIGNS:
        order = z_chunks(s)
        for c in order[:2]:
            add(("rz", 4, s, c), Z, s, 16, [("cr", 4)])
        for d in (3, 2, 1):
            for c in order[2:] + order[:2]:
                before = [] if d == 3 and c in order[2:] else [("rz", d + 1, s, c)]
                add(("rz", d, s, c), Z, s, 16, [("cr", s * d % 8)] + before)
    for h in (0, 1):
        p, q = h, 1 - h
        for s in SIGNS:
            for j in JS:
                add(("r1", h, s, 0, j), q, s, 16, ["ig2"])
                add(("r1", h, s, 1, j), q, s, 16, [("ig1", h)])
                add(("r1", h, s, 2, j), q, s, 16, [("ig1", h), ("r1", h, s, 0, j)])
        for n, s in enumerate(SIGNS):
            line = lambda j, u: ["ig0", ("r1", h, SIGNS[u], 2, j), ("r1", h, SIGNS[1 - u], 1, j)]
            add(("r2", h, s, 0), p, s, 16, line(2, n))
            add(("r2", h, s, 1), p, s, 16, line(s % 4, 1 - n))
            add(("r2", h, s, 2), p, s, 16, line(s % 4, n) + [("r2", h, s, 0)])
    add("loss", None, 0, 0, list(cover.values()))
    for d in (1, 2, 3):
        add(("lx", d), X, d, 2, ["loss"])
    for d in (1, 2, 3):
        add(("ly", d), Y, d, 2, [("lx", e) for e in (1, 2, 3)])
    add("out_rep", None, 0, 0, [("cr", 0)] + [("rz", 1, s, c) for s in SIGNS for c in range(4)])
    lines = [("r1", h, s, k, 0) for h in (0, 1) for s in SIGNS for k in (1, 2)]
    add("out_img", None, 0, 0, ["ig0"] + lines + [("r2", h, s, k) for h in (0, 1) for s in SIGNS for k in (1, 2)])
    add("out_loss", None, 0, 0, [("ly", d) for d in (1, 2, 3)])
    return steps


ORDER = [
    60, 61, 74, 75, 0, 3, 30, 33, 62, 76, 1, 2, 32, 31, 6, 9, 36, 39, 88, 63, 77, 38, 37, 8, 7, 64, 78, 4, 5, 34, 35,
    15, 18, 48, 45, 44, 49, 14, 19, 65, 79, 42, 51, 12, 21, 66, 80, 40, 41, 10, 11, 67, 90, 81, 89, 50, 43, 20, 13,
    68, 82, 54, 57, 24, 27, 69, 83, 52, 55, 22, 17, 70, 84, 56, 47, 26, 25, 71, 92, 85, 91, 46, 53, 16, 23, 72, 86,
    96, 73, 87, 97, 28, 29, 58, 59, 93, 94, 98, 95, 99, 101, 100, 106, 110, 117, 102, 146, 158, 176, 118, 119, 132,
    133, 188, 149, 152, 161, 164, 179, 182, 191, 194, 155, 167, 185, 197, 107, 111, 112, 103, 147, 148, 159, 120, 121,
    122, 134, 135, 136, 160, 150, 162, 151, 104, 123, 137, 177, 178, 189, 190, 153, 163, 154, 165, 166, 180, 192, 108,
    113, 114, 181, 183, 193, 195, 156, 157, 168, 169, 184, 105, 124, 125, 126, 138, 139, 140, 170, 173, 196, 200, 203,
    171, 127, 198, 206, 207, 208, 209, 141, 174, 186, 109, 115, 116, 187, 199, 201, 204, 175, 202, 128, 129, 172, 142,
    143, 205, 130, 144, 210, 211, 212, 131, 145, 214, 215, 213,
]


def my_coords():
    i, t = lax.axis_index("img"), lax.axis_index("txt")
    x, z_hi = lax.rem(t, 4), lax.div(t, 4)
    y, z_lo, c = lax.div(i, 4), lax.rem(lax.div(i, 2), 2), lax.rem(i, 2)
    return (x, y, z_hi * 2 + z_lo, c)


def device_at(co, axis, step):
    co = list(co)
    co[axis] = lax.rem(co[axis] + step + SIZES[axis], SIZES[axis])
    x, y, z, c = co
    return (y * 4 + lax.rem(z, 2) * 2 + c, lax.div(z, 2) * 4 + x)


def unit_rows(ref):
    wide = ref[...].astype(F32)
    inverse = lax.rsqrt(jnp.sum(wide * wide, axis=1, keepdims=True) + 1e-06)
    return wide * inverse, inverse


def project_back(grads, unit_wide, inverse):
    return inverse * (grads - unit_wide * jnp.sum(unit_wide * grads, axis=1, keepdims=True))


def kernel(
    img_ref, rep_ref, gimg_ref, grep_ref, loss_ref,
    own_img, own_rep, ibuf, rbuf, slopes, above, below, gr, ga1, gy,
    st_c, ld_c, st_z, ld_z, st1, ld1, st2, ld2, lb_s, lb_l, lw_s, lw_l,
    ssem, rsem, own_sem,
):
    me = my_coords()
    peers = [(X, 1), (X, -1), (X, 2), (Y, 1), (Y, -1), (Y, 2), (Z, 1), (Z, -1), (C, 1)]
    barrier = pltpu.get_barrier_semaphore()
    for axis, step in peers:
        pl.semaphore_signal(barrier, inc=1, device_id=device_at(me, axis, step), device_id_type=MESH)
    loads = [
        pltpu.make_async_copy(img_ref, own_img, own_sem.at[0]),
        pltpu.make_async_copy(rep_ref, own_rep, own_sem.at[1]),
    ]
    for load in loads:
        load.start()
    above[...] = jnp.zeros_like(above)
    below[...] = jnp.zeros_like(below)
    lb_s[...] = jnp.zeros_like(lb_s)
    for load in loads:
        load.wait()
    ibuf[0] = unit_rows(own_img)[0].astype(BF16)
    rbuf[0, 0] = unit_rows(own_rep)[0].astype(BF16)
    pl.semaphore_wait(barrier, len(peers))

    def quarter(n, count=1):
        return pl.ds(n * 16, count * 16)

    matched = jnp.logical_and(me[Y] == lax.div(me[Z], 2), me[X] == lax.rem(me[Z], 2) * 2 + me[C])
    aside = jnp.where(matched, 0, 1 << 20)
    row_in = lax.broadcasted_iota(jnp.int32, (64, 1), 0)
    col_in = lax.broadcasted_iota(jnp.int32, (1, 128), 1)

    def tile(i, ni, r, nr):
        m = ni * 64
        lhs = ibuf[i : i + ni].reshape(m, D)
        rhs = rbuf[r : r + nr].reshape(nr * 128, D)
        dots = lax.dot_general(lhs, rhs, (((1,), (1,)), ((), ())), preferred_element_type=F32)
        row_ids = []
        for dx, dy in IMG_AT[i : i + ni]:
            block = lax.rem(me[Y] + dy, 4) * 4 + lax.rem(me[X] + dx, 4)
            row_ids.append(block * 64 + aside + row_in)
        row_ids = jnp.concatenate(row_ids, axis=0)
        high = above[i : i + ni].reshape(m, 128)
        low = below[i : i + ni].reshape(m, 128)
        for k in range(nr):
            bz = lax.rem(me[Z] + REP_AT[r + k], 8) * 2
            mine, other = (bz + me[C]) * 64, (bz + 1 - me[C]) * 64
            col_ids = jnp.where(col_in < 64, mine + col_in, other + col_in - 64)
            sign = jnp.where(row_ids == col_ids, -1.0, 1.0)
            bits = (dots[:, k * 128 : k * 128 + 128] * (logit_scale * LOG2E) + logit_bias * LOG2E) * sign
            e = jnp.exp2(-jnp.abs(bits))
            one_e = 1.0 + e
            inverse = 1.0 / one_e
            slope = jnp.where(bits >= 0, inverse, e * inverse) * sign
            slopes[i : i + ni, :, (r + k) * 128 : (r + k) * 128 + 128] = slope.astype(BF16).reshape(ni, 64, 128)
            high = high + jnp.maximum(bits, 0.0)
            low = low * one_e + e
        above[i : i + ni] = high.reshape(ni, 64, 128)
        below[i : i + ni] = low.reshape(ni, 64, 128)

    def img_terms(pieces):
        lhs = jnp.concatenate([slopes[IMG_POS[at(*n)], quarter(2 * n[0], 2)] for n in pieces], axis=0)
        return logit_scale * jnp.dot(lhs, rbuf[...].reshape(1024, D), preferred_element_type=F32)

    def rep_terms(offsets):
        cols = [slopes[:, :, REP_POS[o] * 128 : REP_POS[o] * 128 + 128].reshape(1024, 128) for o in offsets]
        out = logit_scale * lax.dot_general(
            jnp.concatenate(cols, axis=1), ibuf[...].reshape(1024, D), (((0,), (0,)), ((), ())),
            preferred_element_type=F32,
        )
        for n, o in enumerate(offsets):
            gr[REP_POS[o]] = out[n * 128 : n * 128 + 64]
            st_c[REP_POS[o]] = out[n * 128 + 64 : n * 128 + 128].astype(BF16)

    def far_terms():
        out = img_terms([(h, j, 2) for h in (0, 1) for j in JS])
        for h in (0, 1):
            for k in range(4):
                for n in (0, 1):
                    base = (h * 4 + k) * 32 + n * 16
                    st1[h, n, 0, k] = out[base : base + 16].astype(BF16)

    def near_terms(h):
        out = img_terms([(h, j, s) for s in SIGNS for j in JS])
        for n in (0, 1):
            for k in range(4):
                base = (n * 4 + k) * 32
                quarters = [out[base : base + 16], out[base + 16 : base + 32]]
                st1[h, n, 1, k] = quarters[1 - n].astype(BF16)
                ga1[h, n, k] = quarters[n]

    def line_terms():
        out = img_terms([(h, j, 0) for h in (0, 1) for j in JS])
        for h in (0, 1):
            for k in range(4):
                gy[h, k] = out[(h * 4 + k) * 32 : (h * 4 + k) * 32 + 32]

    def line_sum(h, j, u):
        k = JS.index(j)
        total = gy[h, k, quarter(u)] + ld1[h, u, 2, k].astype(F32)
        return total + ld1[h, 1 - u, 1, k].astype(F32)

    def paired(o, c):
        return gr[REP_POS[o % 8], quarter(c)] + ld_c[REP_POS[o % 8], quarter(c)].astype(F32)

    def losses():
        for k in range(8):
            wide = above[2 * k : 2 * k + 2] * LN2 + jnp.log1p(below[2 * k : 2 * k + 2])
            line = jnp.sum(wide.reshape(128, 128).T, axis=0, keepdims=True)
            for n in (0, 1):
                dx, dy = IMG_AT[2 * k + n]
                lb_s[dx, dy : dy + 1, :] = line if n == 0 else pltpu.roll(line, 64, 1)

    def x_losses():
        lw_s[...] = lb_s[0] + lb_l[1] + lb_l[2] + lb_l[3]

    def out_rep():
        parts = [paired(0, c) + ld_z[0, 0, c].astype(F32) + ld_z[1, 0, c].astype(F32) for c in range(4)]
        unit, inverse = unit_rows(own_rep)
        grep_ref[...] = project_back(jnp.concatenate(parts, axis=0), unit, inverse)

    def out_img():
        parts = [
            line_sum(h, 0, u) + ld2[h, u, 2].astype(F32) + ld2[h, 1 - u, 1].astype(F32)
            for h in (0, 1)
            for u in (0, 1)
        ]
        unit, inverse = unit_rows(own_img)
        gimg_ref[...] = project_back(jnp.concatenate(parts, axis=0), unit, inverse)

    def out_loss():
        loss = lw_s[0:1, :]
        for d in (1, 2, 3):
            loss = loss + lw_l[d, d : d + 1, :]
        loss_ref[...] = jnp.broadcast_to(loss, loss_ref.shape)

    compute = {
        "tile": tile, "ig2": far_terms, "ig1": near_terms, "ig0": line_terms,
        "rg": lambda d: rep_terms([4, 0] if d == 4 else [d, 8 - d]),
        "loss": losses, "out_rep": out_rep, "out_img": out_img, "out_loss": out_loss,
    }

    def img_ends(o, part, axis, s):
        return ibuf.at[IMG_POS[o], part], ibuf.at[IMG_POS[shift(o, axis, -s)], part]

    def ends(name):
        kind, a = name[0], name[1:]
        if kind == "g1":
            h, s, u = a
            return img_ends((0, 0), quarter(2 * h + u), h, s)
        if kind == "g2":
            h, s = a
            return img_ends(shift((0, 0), h, -s), quarter(2 * h + SIGNS.index(s)), h, s)
        if kind == "g3":
            h, s, j, u = a
            return img_ends(at(h, j, 0), quarter(2 * h + u), 1 - h, s)
        if kind == "g4":
            h, s, j = a
            return img_ends(at(h, j, -s), quarter(2 * h + SIGNS.index(s)), 1 - h, s)
        if kind == "z":
            d, s, c = a
            return (
                rbuf.at[REP_POS[-s * (d - 1) % 8], 0, quarter(c)],
                rbuf.at[REP_POS[-s * d % 8], 0, quarter(c)],
            )
        if kind == "cg":
            return rbuf.at[REP_POS[a[0]], 0], rbuf.at[REP_POS[a[0]], 1]
        if kind == "cr":
            return st_c.at[REP_POS[a[0]]], ld_c.at[REP_POS[a[0]]]
        if kind == "rz":
            d, s, c = a
            return st_z.at[SIGNS.index(s), d - 1, c], ld_z.at[SIGNS.index(s), d - 1, c]
        if kind == "r1":
            h, s, slot, j = a
            where = (h, SIGNS.index(s), slot, JS.index(j))
            return st1.at[where], ld1.at[where]
        if kind == "r2":
            h, s, slot = a
            return st2.at[h, SIGNS.index(s), slot], ld2.at[h, SIGNS.index(s), slot]
        if kind == "lx":
            return lb_s.at[a[0]], lb_l.at[a[0]]
        return lw_s, lw_l.at[a[0]]

    def prepare(name):
        kind, a = name[0], name[1:]
        if kind == "rz":
            d, s, c = a
            n = SIGNS.index(s)
            term = paired(s * d, c)
            if d < 3 or (d == 3 and c in z_chunks(s)[:2]):
                term = term + ld_z[n, d, c].astype(F32)
            st_z[n, d - 1, c] = term.astype(BF16)
        if kind == "r1" and a[2] == 2:
            h, s, _, j = a
            n, k = SIGNS.index(s), JS.index(j)
            st1[h, n, 2, k] = (ga1[h, n, k] + ld1[h, n, 0, k].astype(F32)).astype(BF16)
        if kind == "r2":
            h, s, slot = a
            n = SIGNS.index(s)
            term = line_sum(h, 2 if slot == 0 else s % 4, 1 - n if slot == 1 else n)
            if slot == 2:
                term = term + ld2[h, n, 0].astype(F32)
            st2[h, n, slot] = term.astype(BF16)
        if name == ("ly", 1):
            x_losses()

    steps = plan()
    copies = {}
    for name, axis, step, _, _ in steps:
        if axis is not None:
            k = len(copies)
            src, dst = ends(name)
            copies[name] = pltpu.make_async_remote_copy(
                src, dst, ssem.at[k], rsem.at[k], device_id=device_at(me, axis, step), device_id_type=MESH
            )
    arrived = set()
    for n in ORDER:
        name, axis, _, _, needs = steps[n]
        for need in needs:
            if need in copies and need not in arrived:
                copies[need].wait_recv()
                arrived.add(need)
        if axis is None:
            args = () if isinstance(name, str) else name[1:]
            compute[name if isinstance(name, str) else name[0]](*args)
        else:
            prepare(name)
            copies[name].start()
    for copy in copies.values():
        copy.wait_send()


def finish(gimg, grep, loss, out_img, out_rep, out_loss, sem):
    stores = [pltpu.make_async_copy(gimg, out_img, sem.at[0]), pltpu.make_async_copy(grep, out_rep, sem.at[1])]
    for store in stores:
        store.start()
    out_loss[...] = loss[0, :64]
    for store in stores:
        store.wait()


COPIES = sum(step[1] is not None for step in plan())


def on_device(image_emb, report_emb):
    vmem = pl.BlockSpec(memory_space=pltpu.VMEM)
    hbm = pl.BlockSpec(memory_space=pl.ANY)
    sums = (
        jax.ShapeDtypeStruct((64, D), F32),
        jax.ShapeDtypeStruct((64, D), F32),
        jax.ShapeDtypeStruct((8, 128), F32),
    )
    gimg, grep, loss = pl.pallas_call(
        kernel,
        out_shape=(pltpu.VMEM((64, D), F32), pltpu.VMEM((64, D), F32), pltpu.VMEM((8, 128), F32)),
        in_specs=[pl.BlockSpec(memory_space=pltpu.HBM)] * 2,
        out_specs=(vmem, vmem, vmem),
        scratch_shapes=[
            pltpu.VMEM((64, D), BF16),
            pltpu.VMEM((64, D), BF16),
            pltpu.VMEM((16, 64, D), BF16),
            pltpu.VMEM((8, 2, 64, D), BF16),
            pltpu.VMEM((16, 64, 1024), BF16),
            pltpu.VMEM((16, 64, 128), F32),
            pltpu.VMEM((16, 64, 128), F32),
            pltpu.VMEM((8, 64, D), F32),
            pltpu.VMEM((2, 2, 4, 16, D), F32),
            pltpu.VMEM((2, 4, 32, D), F32),
            pltpu.VMEM((8, 64, D), BF16),
            pltpu.VMEM((8, 64, D), BF16),
            pltpu.VMEM((2, 4, 4, 16, D), BF16),
            pltpu.VMEM((2, 4, 4, 16, D), BF16),
            pltpu.VMEM((2, 2, 3, 4, 16, D), BF16),
            pltpu.VMEM((2, 2, 3, 4, 16, D), BF16),
            pltpu.VMEM((2, 2, 3, 16, D), BF16),
            pltpu.VMEM((2, 2, 3, 16, D), BF16),
            pltpu.VMEM((4, 8, 128), F32),
            pltpu.VMEM((4, 8, 128), F32),
            pltpu.VMEM((8, 128), F32),
            pltpu.VMEM((4, 8, 128), F32),
            pltpu.SemaphoreType.DMA((COPIES,)),
            pltpu.SemaphoreType.DMA((COPIES,)),
            pltpu.SemaphoreType.DMA((2,)),
        ],
        compiler_params=pltpu.CompilerParams(
            collective_id=0, has_side_effects=True, vmem_limit_bytes=40 * 2**20
        ),
        cost_estimate=pl.CostEstimate(
            flops=3 * 2 * 1024 * 1024 * D, bytes_accessed=900000, transcendentals=3 * 1024 * 1024
        ),
    )(pltpu.with_memory_space_constraint(image_emb, pltpu.HBM), pltpu.with_memory_space_constraint(report_emb, pltpu.HBM))
    return pl.pallas_call(
        finish,
        out_shape=sums[:2] + (jax.ShapeDtypeStruct((64,), F32),),
        in_specs=[vmem, vmem, vmem],
        out_specs=(hbm, hbm, vmem),
        scratch_shapes=[pltpu.SemaphoreType.DMA((2,))],
        compiler_params=pltpu.CompilerParams(vmem_limit_bytes=8 * 2**20),
    )(gimg, grep, loss)


def solution(mesh):
    in_specs = (P(("img", "txt"), None), P(("txt", "img"), None))
    out_specs = (P(("img", "txt"), None), P(("txt", "img"), None), P(("img", "txt")))
    return jax.shard_map(
        on_device, mesh=mesh, in_specs=in_specs, out_specs=out_specs, check_vma=False
    )
```

time: 313 us -> 55.9 us (0.18)
  waiting for transfers between devices: 222 us -> 0 us
  Pallas kernels: 0 us -> 55.1 us
  blocking collectives: 38.2 us -> 0 us
  matrix products: 21.2 us -> 0 us
  between operations: 14.5 us -> 0.64 us
  other arithmetic: 11.4 us -> 0 us
  local copies, waits for them, and re-layouts: 5.48 us -> 0 us
    reduce_scatter x2 -> x0, waiting for transfers between devices: 120 us -> none  [the longest x1 98.6 us: on_device(): lax.psum_scatter(g_img, 'txt', scatter_dimension=0, tiled=True)]
    all_gather x2 -> x0, waiting for transfers between devices: 101 us -> none  [the longest x1 63.2 us: on_device(): all_img = lax.all_gather(send_img, 'txt', axis=0, tiled=True)]
    pallas_call x0 -> x2, Pallas kernels: none -> 55.1 us  [the longest x1 53.8 us: on_device(): pl.pallas_call(kernel, out_shape=(pltpu.VMEM((64, D), F32), pltpu.VMEM((6...]
    unnamed x1 -> x0, blocking collectives: 38.2 us -> none
    dot_general x3 -> x0, matrix products: 21.2 us -> none  [the longest x1 8 us: pair_tile(): lax.dot_general(img_block, rep_block, (((1,), (1,)), ((), ())), preferred...]
    unnamed x14 -> x0, local copies, waits for them, and re-layouts: 5.48 us -> none
    reduce_sum x4 -> x0, other arithmetic: 4.42 us -> none  [the longest x2 2.34 us: project_back(): jnp.sum(unit_wide * grads, axis=1, keepdims=True)]
    mul x2 -> x0, other arithmetic: 3.61 us -> none  [project_back(): inverse * (grads - unit_wide * jnp.sum(unit_wide * grads, axis=1, keepdim...]
  transfers between devices with their start and end apart: 4 -> 0, of which waited for: 4 -> 0; matrix products, arithmetic and copies ran while one was open for 5% -> 0% of each run, Pallas kernels for 0% -> 0%
where the time goes in v2:
time: 55.9 us; the launch traced here: 55.8 us
  Pallas kernels  55.1 us (99%)
  between operations  0.64 us (1%)
    pallas_call x1, Pallas kernels, on_device(): pl.pallas_call(kernel, out_shape=(pltpu.VMEM((64, D), F32), pltpu.VMEM((6...  53.8 us
    pallas_call x1, Pallas kernels, on_device(): pl.pallas_call(finish, out_shape=sums[:2] + (jax.ShapeDtypeStruct((64,),...  1.34 us

profile of v2, /device:TPU:1, one launch (start us, length us, event | category | flops | bytes accessed | tf_op | source)
XLA Modules:
  0.0 55.8 jit_solution(15839682103877026912)
XLA Ops:
  0.6 53.8 %shard_map.49 = (f32[64,1152]{1,0:T(8,128)S(1)}, f32[64,1152]{1,0:T(8,128)S(1)}, f32[8,128]{1,0:T(8,128)S(1)}) custom-call(bf16[64,1152]{1,0:T(8,128)(2,1)} %img_ref.1, bf16[64,1152]{1,0:T(8,128)(2,1)} %rep_ref.1), custom_call_target="tpu_custom_call" | custom-call | flops 7247757312 | bytes 900000 | tf_op jit(solution)/shard_map/pallas_call | solution.py:417
  54.4 1.3 %shard_map.50 = (f32[64,1152]{1,0:T(8,128)}, f32[64,1152]{1,0:T(8,128)}, f32[64]{0:T(128)}) custom-call(f32[64,1152]{1,0:T(8,128)S(1)} %get-tuple-element.6.gimg, f32[64,1152]{1,0:T(8,128)S(1)} %get-tuple-element.7.grep, f32[8,128]{1,0:T(8,128)S(1)} %get-tuple-element.8.loss), custom_call_target="tpu_custom_call" | custom-call | tf_op jit(solution)/shard_map/pallas_call | solution.py:456

commit v3 on v2

--- a/solution.py
+++ b/solution.py
@@ -22,7 +22,7 @@
 IMG_POS = {o: n for n, o in enumerate(IMG_AT)}
 REP_POS = {o: n for n, o in enumerate(REP_AT)}
 JS = (2, 1, 3, 0)
-TILES = [(0, 4, 0, 4), (4, 4, 0, 4), (0, 8, 4, 2), (8, 4, 0, 6), (0, 12, 6, 2), (12, 4, 0, 8)]
+TILES = [(0, 5, 0, 3), (5, 5, 0, 3), (0, 10, 3, 2), (10, 3, 0, 5), (0, 13, 5, 2), (13, 3, 0, 5), (13, 3, 5, 3), (0, 13, 7, 1)]
 
 
 def shift(o, axis, by):
@@ -123,16 +123,18 @@
     return steps
 
 
+SENDS = ("g1", "g2", "g3", "g4", "z", "cg", "cr", "rz", "r1", "r2", "lx", "ly")
+
 ORDER = [
-    60, 61, 74, 75, 0, 3, 30, 33, 62, 76, 1, 2, 32, 31, 6, 9, 36, 39, 88, 63, 77, 38, 37, 8, 7, 64, 78, 4, 5, 34, 35,
-    15, 18, 48, 45, 44, 49, 14, 19, 65, 79, 42, 51, 12, 21, 66, 80, 40, 41, 10, 11, 67, 90, 81, 89, 50, 43, 20, 13,
-    68, 82, 54, 57, 24, 27, 69, 83, 52, 55, 22, 17, 70, 84, 56, 47, 26, 25, 71, 92, 85, 91, 46, 53, 16, 23, 72, 86,
-    96, 73, 87, 97, 28, 29, 58, 59, 93, 94, 98, 95, 99, 101, 100, 106, 110, 117, 102, 146, 158, 176, 118, 119, 132,
-    133, 188, 149, 152, 161, 164, 179, 182, 191, 194, 155, 167, 185, 197, 107, 111, 112, 103, 147, 148, 159, 120, 121,
-    122, 134, 135, 136, 160, 150, 162, 151, 104, 123, 137, 177, 178, 189, 190, 153, 163, 154, 165, 166, 180, 192, 108,
-    113, 114, 181, 183, 193, 195, 156, 157, 168, 169, 184, 105, 124, 125, 126, 138, 139, 140, 170, 173, 196, 200, 203,
-    171, 127, 198, 206, 207, 208, 209, 141, 174, 186, 109, 115, 116, 187, 199, 201, 204, 175, 202, 128, 129, 172, 142,
-    143, 205, 130, 144, 210, 211, 212, 131, 145, 214, 215, 213,
+    0, 61, 60, 74, 75, 3, 39, 30, 38, 31, 6, 33, 88, 2, 62, 77, 1, 32, 7, 36, 63, 76, 37, 8, 9, 4, 65, 18, 78, 19, 5,
+    48, 43, 34, 15, 64, 79, 42, 45, 14, 35, 66, 81, 44, 51, 12, 21, 67, 90, 80, 89, 50, 41, 20, 11, 69, 82, 40, 49,
+    24, 27, 96, 68, 83, 54, 13, 22, 55, 70, 85, 52, 57, 26, 25, 92, 71, 84, 91, 46, 53, 10, 17, 73, 86, 56, 47, 16,
+    23, 28, 29, 72, 87, 58, 98, 59, 94, 93, 97, 99, 95, 100, 101, 103, 102, 108, 119, 112, 104, 154, 166, 148, 190,
+    178, 163, 184, 193, 109, 114, 120, 135, 134, 113, 121, 151, 157, 187, 160, 196, 169, 181, 199, 105, 164, 158, 136,
+    155, 137, 122, 161, 123, 106, 192, 180, 179, 200, 165, 149, 139, 150, 124, 110, 116, 115, 162, 191, 182, 197, 153,
+    186, 168, 138, 125, 152, 111, 198, 167, 183, 185, 194, 140, 127, 126, 156, 117, 118, 159, 171, 143, 208, 209, 195,
+    128, 189, 210, 211, 170, 141, 107, 202, 172, 205, 142, 129, 175, 201, 206, 173, 144, 188, 131, 176, 147, 130, 212,
+    213, 214, 203, 145, 132, 204, 207, 174, 146, 133, 177, 217, 216, 215,
 ]
 
 
@@ -375,7 +377,7 @@
             k = len(copies)
             src, dst = ends(name)
             copies[name] = pltpu.make_async_remote_copy(
-                src, dst, ssem.at[k], rsem.at[k], device_id=device_at(me, axis, step), device_id_type=MESH
+                src, dst, ssem.at[SENDS.index(name[0])], rsem.at[k], device_id=device_at(me, axis, step), device_id_type=MESH
             )
     arrived = set()
     for n in ORDER:
@@ -390,8 +392,15 @@
         else:
             prepare(name)
             copies[name].start()
-    for copy in copies.values():
-        copy.wait_send()
+    sent = {
+        "g1": ibuf.at[pl.ds(0, 2)], "g2": ibuf.at[pl.ds(0, 1)], "g3": ibuf.at[pl.ds(0, 8)], "g4": ibuf.at[pl.ds(0, 4)],
+        "z": rbuf.at[pl.ds(0, 7), 0], "cg": rbuf.at[:, 0], "cr": st_c, "rz": rbuf.at[pl.ds(0, 7), 0],
+        "r1": st1, "r2": st2, "lx": lb_s.at[pl.ds(1, 3)], "ly": lw_l.at[pl.ds(1, 3)],
+    }
+    for n, kind in enumerate(SENDS):
+        pltpu.make_async_remote_copy(
+            sent[kind], sent[kind], ssem.at[n], rsem.at[0], device_id=device_at(me, C, 1), device_id_type=MESH
+        ).wait_send()
 
 
 def finish(gimg, grep, loss, out_img, out_rep, out_loss, sem):
@@ -442,7 +451,7 @@
             pltpu.VMEM((4, 8, 128), F32),
             pltpu.VMEM((8, 128), F32),
             pltpu.VMEM((4, 8, 128), F32),
-            pltpu.SemaphoreType.DMA((COPIES,)),
+            pltpu.SemaphoreType.DMA((len(SENDS),)),
             pltpu.SemaphoreType.DMA((COPIES,)),
             pltpu.SemaphoreType.DMA((2,)),
         ],

time: 55.9 us -> 50.8 us (0.909)
  Pallas kernels: 55.1 us -> 50.1 us
    pallas_call x1, Pallas kernels: 53.8 us -> 48.7 us  [on_device(): pl.pallas_call(kernel, out_shape=(pltpu.VMEM((64, D), F32), pltpu.VMEM((6...]
where the time goes in v3:
time: 50.8 us; the launch traced here: 50.7 us
  Pallas kernels  50.1 us (99%)
  between operations  0.64 us (1%)
    pallas_call x1, Pallas kernels, on_device(): pl.pallas_call(kernel, out_shape=(pltpu.VMEM((64, D), F32), pltpu.VMEM((6...  48.7 us
    pallas_call x1, Pallas kernels, on_device(): pl.pallas_call(finish, out_shape=sums[:2] + (jax.ShapeDtypeStruct((64,),...  1.34 us

profile of v3, /device:TPU:1, one launch (start us, length us, event | category | flops | bytes accessed | tf_op | source)
XLA Modules:
  0.0 50.7 jit_solution(13040520154946689498)
XLA Ops:
  0.6 48.7 %shard_map.49 = (f32[64,1152]{1,0:T(8,128)S(1)}, f32[64,1152]{1,0:T(8,128)S(1)}, f32[8,128]{1,0:T(8,128)S(1)}) custom-call(bf16[64,1152]{1,0:T(8,128)(2,1)} %img_ref.1, bf16[64,1152]{1,0:T(8,128)(2,1)} %rep_ref.1), custom_call_target="tpu_custom_call" | custom-call | flops 7247757312 | bytes 900000 | tf_op jit(solution)/shard_map/pallas_call | solution.py:426
  49.4 1.3 %shard_map.50 = (f32[64,1152]{1,0:T(8,128)}, f32[64,1152]{1,0:T(8,128)}, f32[64]{0:T(128)}) custom-call(f32[64,1152]{1,0:T(8,128)S(1)} %get-tuple-element.6.gimg, f32[64,1152]{1,0:T(8,128)S(1)} %get-tuple-element.7.grep, f32[8,128]{1,0:T(8,128)S(1)} %get-tuple-element.8.loss), custom_call_target="tpu_custom_call" | custom-call | tf_op jit(solution)/shard_map/pallas_call | solution.py:465

commit v4 on v3

--- a/solution.py
+++ b/solution.py
@@ -86,11 +86,11 @@
     for h in (0, 1):
         add(("ig1", h), None, 0, 256, img_tiles([at(h, j, s) for s in SIGNS for j in JS]))
     add("ig0", None, 0, 256, img_tiles([at(h, j, 0) for h in (0, 1) for j in JS]))
-    for d in (4, 3, 2, 1):
-        add(("rg", d), None, 0, 256, rep_tiles([d, 0] if d == 4 else [d, 8 - d]))
+    for d in (4, 3, 2, 1, 0):
+        add(("rg", d), None, 0, 256, rep_tiles([d] if d in (0, 4) else [d, 8 - d]))
     for d in (4, 3, 2, 1, 0):
         for o in (d, 8 - d) if d in (1, 2, 3) else (d,):
-            add(("cr", o), C, 1, 64, [("rg", d or 4)])
+            add(("cr", o), C, 1, 64, [("rg", d)])
     for s in SIGNS:
         order = z_chunks(s)
         for c in order[:2]:
@@ -126,16 +126,21 @@
 SENDS = ("g1", "g2", "g3", "g4", "z", "cg", "cr", "rz", "r1", "r2", "lx", "ly")
 
 ORDER = [
-    0, 61, 60, 74, 75, 3, 39, 30, 38, 31, 6, 33, 88, 2, 62, 77, 1, 32, 7, 36, 63, 76, 37, 8, 9, 4, 65, 18, 78, 19, 5,
-    48, 43, 34, 15, 64, 79, 42, 45, 14, 35, 66, 81, 44, 51, 12, 21, 67, 90, 80, 89, 50, 41, 20, 11, 69, 82, 40, 49,
-    24, 27, 96, 68, 83, 54, 13, 22, 55, 70, 85, 52, 57, 26, 25, 92, 71, 84, 91, 46, 53, 10, 17, 73, 86, 56, 47, 16,
-    23, 28, 29, 72, 87, 58, 98, 59, 94, 93, 97, 99, 95, 100, 101, 103, 102, 108, 119, 112, 104, 154, 166, 148, 190,
-    178, 163, 184, 193, 109, 114, 120, 135, 134, 113, 121, 151, 157, 187, 160, 196, 169, 181, 199, 105, 164, 158, 136,
-    155, 137, 122, 161, 123, 106, 192, 180, 179, 200, 165, 149, 139, 150, 124, 110, 116, 115, 162, 191, 182, 197, 153,
-    186, 168, 138, 125, 152, 111, 198, 167, 183, 185, 194, 140, 127, 126, 156, 117, 118, 159, 171, 143, 208, 209, 195,
-    128, 189, 210, 211, 170, 141, 107, 202, 172, 205, 142, 129, 175, 201, 206, 173, 144, 188, 131, 176, 147, 130, 212,
-    213, 214, 203, 145, 132, 204, 207, 174, 146, 133, 177, 217, 216, 215,
+    60, 61, 74, 75, 0, 3, 30, 33, 31, 32, 1, 2, 88, 62, 76, 36, 39, 6, 9, 63, 77, 38, 37, 8, 7, 64, 78, 4, 5, 34, 35,
+    45, 48, 15, 18, 44, 65, 14, 79, 19, 49, 42, 66, 51, 80, 12, 21, 40, 67, 10, 81, 11, 41, 89, 90, 50, 43, 20, 13,
+    68, 82, 54, 57, 24, 27, 96, 69, 83, 52, 47, 26, 25, 70, 84, 56, 55, 22, 17, 71, 92, 85, 91, 46, 53, 16, 23, 72,
+    86, 98, 73, 87, 58, 28, 29, 59, 97, 94, 93, 99, 100, 95, 101, 110, 116, 117, 103, 102, 108, 113, 104, 149, 161,
+    179, 191, 152, 164, 182, 194, 121, 122, 135, 136, 109, 114, 115, 155, 167, 185, 197, 158, 170, 188, 200, 105, 123,
+    124, 150, 162, 106, 137, 138, 180, 151, 163, 181, 192, 193, 153, 165, 107, 125, 126, 139, 154, 140, 166, 183, 184,
+    195, 209, 210, 211, 212, 156, 168, 196, 111, 127, 157, 169, 186, 198, 118, 187, 119, 112, 128, 141, 199, 159, 171,
+    189, 120, 201, 160, 172, 142, 173, 176, 129, 203, 206, 143, 190, 202, 130, 213, 214, 215, 144, 174, 204, 131, 177,
+    132, 145, 207, 146, 133, 147, 175, 134, 178, 205, 208, 148, 218, 217, 216,
 ]
+
+
+def group_of(name):
+    last = (name[0] == "r2" and name[3] > 0) or (name[0] == "rz" and name[1] == 1) or name[0] in ("lx", "ly")
+    return name[0] if last else name
 
 
 def my_coords():
@@ -231,7 +236,7 @@
     def rep_terms(offsets):
         cols = [slopes[:, :, REP_POS[o] * 128 : REP_POS[o] * 128 + 128].reshape(1024, 128) for o in offsets]
         out = logit_scale * lax.dot_general(
-            jnp.concatenate(cols, axis=1), ibuf[...].reshape(1024, D), (((0,), (0,)), ((), ())),
+            jnp.concatenate(cols, axis=1) if len(cols) > 1 else cols[0], ibuf[...].reshape(1024, D), (((0,), (0,)), ((), ())),
             preferred_element_type=F32,
         )
         for n, o in enumerate(offsets):
@@ -302,7 +307,7 @@
 
     compute = {
         "tile": tile, "ig2": far_terms, "ig1": near_terms, "ig0": line_terms,
-        "rg": lambda d: rep_terms([4, 0] if d == 4 else [d, 8 - d]),
+        "rg": lambda d: rep_terms([d] if d in (0, 4) else [d, 8 - d]),
         "loss": losses, "out_rep": out_rep, "out_img": out_img, "out_loss": out_loss,
     }
 
@@ -372,9 +377,13 @@
 
     steps = plan()
     copies = {}
+    together = {
+        "r2": ibuf.at[pl.ds(0, 2)], "rz": ibuf.at[pl.ds(0, 2)], "lx": lb_s.at[pl.ds(1, 3)], "ly": lw_l.at[pl.ds(1, 3)],
+    }
+    landing = {}
     for name, axis, step, _, _ in steps:
         if axis is not None:
-            k = len(copies)
+            k = landing.setdefault(group_of(name), len(landing))
             src, dst = ends(name)
             copies[name] = pltpu.make_async_remote_copy(
                 src, dst, ssem.at[SENDS.index(name[0])], rsem.at[k], device_id=device_at(me, axis, step), device_id_type=MESH
@@ -383,9 +392,16 @@
     for n in ORDER:
         name, axis, _, _, needs = steps[n]
         for need in needs:
-            if need in copies and need not in arrived:
-                copies[need].wait_recv()
-                arrived.add(need)
+            group = group_of(need)
+            if need in copies and group not in arrived:
+                copy = copies[need]
+                if group in together:
+                    copy = pltpu.make_async_remote_copy(
+                        together[group], together[group], ssem.at[0], rsem.at[landing[group]],
+                        device_id=device_at(me, C, 1), device_id_type=MESH,
+                    )
+                copy.wait_recv()
+                arrived.add(group)
         if axis is None:
             args = () if isinstance(name, str) else name[1:]
             compute[name if isinstance(name, str) else name[0]](*args)
@@ -412,7 +428,7 @@
         store.wait()
 
 
-COPIES = sum(step[1] is not None for step in plan())
+LANDINGS = len({group_of(step[0]) for step in plan() if step[1] is not None})
 
 
 def on_device(image_emb, report_emb):
@@ -452,7 +468,7 @@
             pltpu.VMEM((8, 128), F32),
             pltpu.VMEM((4, 8, 128), F32),
             pltpu.SemaphoreType.DMA((len(SENDS),)),
-            pltpu.SemaphoreType.DMA((COPIES,)),
+            pltpu.SemaphoreType.DMA((LANDINGS,)),
             pltpu.SemaphoreType.DMA((2,)),
         ],
         compiler_params=pltpu.CompilerParams(

time: 50.8 us -> 50.2 us (0.988)
  Pallas kernels: 50.1 us -> 49.5 us
    pallas_call x1, Pallas kernels: 48.7 us -> 48.1 us  [on_device(): pl.pallas_call(kernel, out_shape=(pltpu.VMEM((64, D), F32), pltpu.VMEM((6...]
where the time goes in v4:
time: 50.2 us; the launch traced here: 50.1 us
  Pallas kernels  49.5 us (99%)
  between operations  0.64 us (1%)
    pallas_call x1, Pallas kernels, on_device(): pl.pallas_call(kernel, out_shape=(pltpu.VMEM((64, D), F32), pltpu.VMEM((6...  48.1 us
    pallas_call x1, Pallas kernels, on_device(): pl.pallas_call(finish, out_shape=sums[:2] + (jax.ShapeDtypeStruct((64,),...  1.34 us

profile of v4, /device:TPU:1, one launch (start us, length us, event | category | flops | bytes accessed | tf_op | source)
XLA Modules:
  0.0 50.1 jit_solution(12311101236866090591)
XLA Ops:
  0.6 48.1 %shard_map.49 = (f32[64,1152]{1,0:T(8,128)S(1)}, f32[64,1152]{1,0:T(8,128)S(1)}, f32[8,128]{1,0:T(8,128)S(1)}) custom-call(bf16[64,1152]{1,0:T(8,128)(2,1)} %img_ref.1, bf16[64,1152]{1,0:T(8,128)(2,1)} %rep_ref.1), custom_call_target="tpu_custom_call" | custom-call | flops 7247757312 | bytes 900000 | tf_op jit(solution)/shard_map/pallas_call | solution.py:442
  48.8 1.3 %shard_map.50 = (f32[64,1152]{1,0:T(8,128)}, f32[64,1152]{1,0:T(8,128)}, f32[64]{0:T(128)}) custom-call(f32[64,1152]{1,0:T(8,128)S(1)} %get-tuple-element.6.gimg, f32[64,1152]{1,0:T(8,128)S(1)} %get-tuple-element.7.grep, f32[8,128]{1,0:T(8,128)S(1)} %get-tuple-element.8.loss), custom_call_target="tpu_custom_call" | custom-call | tf_op jit(solution)/shard_map/pallas_call | solution.py:481

commit v5 on v4

--- a/solution.py
+++ b/solution.py
@@ -126,15 +126,15 @@
 SENDS = ("g1", "g2", "g3", "g4", "z", "cg", "cr", "rz", "r1", "r2", "lx", "ly")
 
 ORDER = [
-    60, 61, 74, 75, 0, 3, 30, 33, 31, 32, 1, 2, 88, 62, 76, 36, 39, 6, 9, 63, 77, 38, 37, 8, 7, 64, 78, 4, 5, 34, 35,
-    45, 48, 15, 18, 44, 65, 14, 79, 19, 49, 42, 66, 51, 80, 12, 21, 40, 67, 10, 81, 11, 41, 89, 90, 50, 43, 20, 13,
-    68, 82, 54, 57, 24, 27, 96, 69, 83, 52, 47, 26, 25, 70, 84, 56, 55, 22, 17, 71, 92, 85, 91, 46, 53, 16, 23, 72,
-    86, 98, 73, 87, 58, 28, 29, 59, 97, 94, 93, 99, 100, 95, 101, 110, 116, 117, 103, 102, 108, 113, 104, 149, 161,
-    179, 191, 152, 164, 182, 194, 121, 122, 135, 136, 109, 114, 115, 155, 167, 185, 197, 158, 170, 188, 200, 105, 123,
-    124, 150, 162, 106, 137, 138, 180, 151, 163, 181, 192, 193, 153, 165, 107, 125, 126, 139, 154, 140, 166, 183, 184,
-    195, 209, 210, 211, 212, 156, 168, 196, 111, 127, 157, 169, 186, 198, 118, 187, 119, 112, 128, 141, 199, 159, 171,
-    189, 120, 201, 160, 172, 142, 173, 176, 129, 203, 206, 143, 190, 202, 130, 213, 214, 215, 144, 174, 204, 131, 177,
-    132, 145, 207, 146, 133, 147, 175, 134, 178, 205, 208, 148, 218, 217, 216,
+    30, 61, 74, 75, 3, 0, 77, 1, 60, 62, 33, 31, 32, 39, 6, 9, 36, 63, 76, 8, 37, 38, 2, 88, 7, 34, 48, 65, 78, 5, 4,
+    18, 15, 14, 49, 35, 44, 45, 19, 51, 64, 79, 50, 12, 13, 42, 43, 10, 66, 81, 11, 40, 41, 90, 67, 80, 89, 21, 20,
+    96, 69, 26, 82, 54, 27, 52, 55, 17, 22, 24, 68, 25, 83, 57, 56, 70, 85, 47, 16, 71, 84, 53, 92, 91, 46, 23, 97,
+    73, 86, 98, 58, 72, 29, 87, 59, 28, 94, 93, 99, 100, 95, 101, 103, 102, 108, 113, 104, 149, 161, 179, 191, 185,
+    194, 152, 182, 197, 164, 167, 158, 155, 170, 188, 200, 135, 122, 136, 121, 109, 115, 114, 209, 211, 212, 210, 105,
+    162, 150, 156, 168, 106, 201, 186, 123, 124, 192, 198, 138, 180, 183, 159, 137, 165, 110, 193, 181, 151, 117, 163,
+    195, 153, 116, 189, 139, 126, 171, 107, 166, 140, 125, 187, 196, 154, 111, 213, 184, 199, 169, 118, 119, 214, 160,
+    215, 112, 190, 202, 120, 172, 157, 127, 142, 128, 141, 130, 143, 173, 176, 203, 206, 129, 144, 218, 174, 207, 204,
+    131, 146, 132, 145, 177, 134, 147, 175, 178, 205, 208, 133, 148, 217, 216,
 ]
 
 

time: 50.2 us -> 50.5 us (level)
  no operation moved by 1% of the time
where the time goes in v5:
time: 50.5 us; the launch traced here: 50.4 us
  Pallas kernels  49.8 us (99%)
  between operations  0.64 us (1%)
    pallas_call x1, Pallas kernels, on_device(): pl.pallas_call(kernel, out_shape=(pltpu.VMEM((64, D), F32), pltpu.VMEM((6...  48.4 us
    pallas_call x1, Pallas kernels, on_device(): pl.pallas_call(finish, out_shape=sums[:2] + (jax.ShapeDtypeStruct((64,),...  1.34 us

profile of v5, /device:TPU:1, one launch (start us, length us, event | category | flops | bytes accessed | tf_op | source)
XLA Modules:
  0.0 50.4 jit_solution(10400037343159715004)
XLA Ops:
  0.6 48.4 %shard_map.49 = (f32[64,1152]{1,0:T(8,128)S(1)}, f32[64,1152]{1,0:T(8,128)S(1)}, f32[8,128]{1,0:T(8,128)S(1)}) custom-call(bf16[64,1152]{1,0:T(8,128)(2,1)} %img_ref.1, bf16[64,1152]{1,0:T(8,128)(2,1)} %rep_ref.1), custom_call_target="tpu_custom_call" | custom-call | flops 7247757312 | bytes 900000 | tf_op jit(solution)/shard_map/pallas_call | solution.py:442
  49.1 1.3 %shard_map.50 = (f32[64,1152]{1,0:T(8,128)}, f32[64,1152]{1,0:T(8,128)}, f32[64]{0:T(128)}) custom-call(f32[64,1152]{1,0:T(8,128)S(1)} %get-tuple-element.6.gimg, f32[64,1152]{1,0:T(8,128)S(1)} %get-tuple-element.7.grep, f32[8,128]{1,0:T(8,128)S(1)} %get-tuple-element.8.loss), custom_call_target="tpu_custom_call" | custom-call | tf_op jit(solution)/shard_map/pallas_call | solution.py:481
